TPU v7x, 32 devices: a whole 2x2x4 slice. The times are simulated.
32 devices in a mesh: vrow: 8 (over z, x), aux: 2 (over y), grp: 2 (over core).
Axes of the slice: x: 2, y: 2, z: 4, core: 2. Of those that a mesh axis runs over, the one named last changes fastest.
Arguments:
- trials: bfloat16 [192, 3840], P(None, 'vrow'), may hold values from -6 to 6
- vv_factors: bfloat16 [16, 3840, 3840], P(('aux', 'grp'), 'vrow'), may hold values from -0.09375 to 0.09375
- screened: bfloat16 [16, 96, 96], P(('aux', 'grp')), may hold values from -0.15625 to 0.15625
- ov_factors: bfloat16 [16, 3840, 96], P(('aux', 'grp'), 'vrow'), may hold values from -0.078125 to 0.078125
- occ_energy: float32 [96], replicated, may hold values from -1.5 to -0.3
- virt_energy: float32 [3840], replicated, may hold values from 0.2 to 2.5
- occ_order: int32 [96], replicated, may hold values from 0 to 95, each once
- virt_order: int32 [3840], P('vrow'), may hold values from 0 to 3839, each once
Outputs:
- sigma: float32 [192, 3840], P(('aux', 'grp'), 'vrow')
Inputs may be any that keep to these rules, and one draw needn't show every extreme that they name: `occ_order`: each active occupied orbital names a different entry. `virt_order`: each virtual orbital names a different entry.
All inputs are finite; a program needn't handle non-finite values.
Results may differ from a plain program's by a relative error of at most 0.0022.
Values may be sent and summed in bfloat16 or wider, within the bound.
A program may use at most 64 MiB of HBM per device.

v0:
```python
import jax
import jax.numpy as jnp
from jax import lax
from jax.sharding import PartitionSpec as P


def table_lookup(order, table):
    columns = lax.broadcasted_iota(jnp.int32, (order.shape[0], table.shape[0]), 1)
    picker = (order[:, None] == columns).astype(jnp.float32)
    return jnp.dot(picker, table, precision=lax.Precision.HIGHEST)


def on_device(
    trials, vv_factors, screened, ov_factors, occ_energy, virt_energy, occ_order, virt_order
):
    groups = lax.axis_size(("aux", "grp"))
    rows_all = trials.shape[0]
    occupied = occ_energy.shape[0]
    count_trials = rows_all // occupied
    local_virt = trials.shape[1]
    slab_count = vv_factors.shape[0]
    row_share = rows_all // groups
    row_offset = lax.axis_index(("aux", "grp")) * row_share
    split_trials = trials.reshape(count_trials, occupied, local_virt)
    partial_pairs = jnp.einsum(
        "qai,tia->qt", ov_factors, split_trials, preferred_element_type=jnp.float32
    )
    pair_sums = lax.psum(partial_pairs, "vrow")
    exchange_term = 2.0 * jnp.einsum("qai,qt->tia", ov_factors.astype(jnp.float32), pair_sums)
    products = jnp.einsum(
        "rb,qab->qra",
        lax.all_gather(trials, "vrow", axis=1, tiled=True),
        vv_factors,
        preferred_element_type=jnp.float32,
    )
    rounded = products.astype(jnp.bfloat16).reshape(slab_count, count_trials, occupied, local_virt)
    direct_term = jnp.einsum("qji,qtja->tia", screened, rounded, preferred_element_type=jnp.float32)
    combined = (exchange_term - direct_term).reshape(rows_all, local_virt)
    summed = lax.psum_scatter(combined, ("aux", "grp"), scatter_dimension=0, tiled=True)
    virt_levels = table_lookup(virt_order, virt_energy)
    occ_levels = table_lookup(occ_order, occ_energy)
    row_ids = row_offset + lax.broadcasted_iota(jnp.int32, (row_share,), 0)
    row_levels = table_lookup(row_ids % occupied, occ_levels)
    own_trials = lax.dynamic_slice_in_dim(trials, row_offset, row_share, 0).astype(jnp.float32)
    return summed + (virt_levels[None, :] - row_levels[:, None]) * own_trials


def solution(mesh):
    placed = (
        P(None, "vrow"),
        P(("aux", "grp"), "vrow", None),
        P(("aux", "grp"), None, None),
        P(("aux", "grp"), "vrow", None),
        P(),
        P(),
        P(),
        P("vrow"),
    )
    return jax.shard_map(
        on_device, mesh=mesh, in_specs=placed, out_specs=P(("aux", "grp"), "vrow"), check_vma=False
    )
```

profile of v0, /device:TPU:0, one launch (start us, length us, event | category | flops | bytes accessed | tf_op | source)
XLA Modules:
  0.0 99.1 jit_solution(16760670691183193712)
XLA Ops:
  6.5 0.0 copy-start
  6.5 0.0 all-gather.3.cloned.1.call-start
  6.5 0.7 all-gather.3.cloned.1.call-update
  7.3 0.0 reduce-scatter.2.cloned.1.call-start
  7.3 1.7 %convolution_bitcast_fusion.1 = f32[4,2]{0,1:T(2,128)S(1)} fusion(bf16[4,480,96]{1,2,0:T(8,128)(2,1)} %param.11, bf16[2,96,480]{2,1,0:T(8,128)(2,1)} %bitcast.41), kind=kOutput, calls=%fused_computation.8 | convolution fusion | flops 737280 | bytes 552992 | tf_op jit(solution)/shard_map/qai,tia->qt/dot_general | solution.py:25
  9.1 23.2 %psum.7 = bf16[4,2]{0,1:T(2,128)(2,1)S(1)} all-reduce(f32[4,2]{0,1:T(2,128)S(1)} %convolution_bitcast_fusion.1), channel_id=1, replica_groups=mesh['vrow'=8,'aux'=2,'grp'=2] {'vrow'}, use_global_device_ids=true, to_apply=%region_0.0 | all-reduce | flops 8 | bytes 48 | tf_op jit(solution)/shard_map/psum | solution.py:28
  32.3 24.2 %all-gather.3.cloned.1.call-done = bf16[8,480,192]{1,2,0:T(8,128)(2,1)} async-done(((bf16[1,480,192]{1,2,0:T(8,128)(2,1)}), bf16[8,480,192]{1,2,0:T(8,128)(2,1)}) %all-gather.3.cloned.1.call-update) | async-done | bytes 1474576 | tf_op jit(solution)/shard_map/all_gather | solution.py:32
  56.5 2.3 %copy.23 = bf16[8,480,192]{1,0,2:T(8,128)(2,1)S(1)} copy(bf16[8,480,192]{1,2,0:T(8,128)(2,1)} %all-gather.3.cloned.1.call-done) | data formatting | bytes 2949120 | tf_op jit(solution)/shard_map/all_gather | solution.py:32
  58.8 2.4 %reshape.30 = bf16[3840,192,1]{0,1,2:T(8,128)(2,1)S(1)} reshape(bf16[8,480,192]{1,0,2:T(8,128)(2,1)S(1)} %copy.23) | data formatting | bytes 2949120
  61.2 0.0 copy-start.2
  61.2 7.8 %convolution_convert_fusion = bf16[4,480,192]{1,2,0:T(8,128)(2,1)S(1)} fusion(bf16[4,480,3840]{2,1,0:T(8,128)(2,1)} %param.9, bf16[3840,192,1]{0,1,2:T(8,128)(2,1)S(1)} %reshape.30), kind=kOutput, calls=%fused_computation.3 | convolution fusion | flops 2831523840 | bytes 16957440 | tf_op jit(solution)/shard_map/rb,qab->qra/dot_general | solution.py:30
  69.0 0.0 copy-done
  69.0 0.3 convolution_bitcast_fusion
  69.3 0.0 copy-done.2
  69.3 0.0 copy-start.1
  69.4 0.0 copy-start.4
  69.4 0.0 copy-start.5
  69.4 0.0 copy-start.3
  69.4 0.6 fusion.3
  70.0 0.8 copy.26
  70.8 0.0 reduce-scatter.2.cloned.1.call-update
  70.8 0.0 copy-done.1
  70.9 0.0 copy-done.4
  70.9 0.0 copy-done.5
  70.9 0.2 convolution_bitcast_fusion.3
  71.1 0.2 convolution_bitcast_fusion.2
  71.3 0.0 copy-done.3
  71.3 3.4 %fusion = f32[1,480]{1,0:T(1,128)S(1)} fusion(f32[3840,1]{0,1:T(1,128)S(1)} %reshape.33, s32[480]{0:T(512)S(1)} %copy-done.3), kind=kOutput, calls=%fused_computation.1 | convolution fusion | flops 23961600 | bytes 19200 | tf_op jit(solution)/shard_map/dot_general | solution.py:10
  74.7 15.9 %reduce-scatter.2.cloned.1.call-done = f32[48,480]{1,0:T(8,128)} async-done(((f32[192,480]{1,0:T(8,128)}), f32[48,480]{1,0:T(8,128)}) %reduce-scatter.2.cloned.1.call-update) | async-done | bytes 92176 | tf_op jit(solution)/shard_map/reduce_scatter | solution.py:39
  90.6 1.6 %multiply_add_fusion = f32[48,480]{1,0:T(8,128)} fusion(f32[48,480]{1,0:T(8,128)} %reduce-scatter.2.cloned.1.call-done, bf16[192,480]{1,0:T(8,128)(2,1)} %param.8, s32[]{:T(128)S(6)} %select_n.15, f32[48]{0:T(128)S(1)} %convolution_bitcast_fusion.2, f32[480]{0:T(512)S(1)} %bitcast.42), kind=kLoop, calls=%fused_computation.15 | loop fusion | flops 92160 | bytes 232516 | tf_op jit(solution)/shard_map/add | solution.py:45
  (2 shorter events, 0.0 us)
Async XLA Ops:
  6.5 62.5 %copy-start = (bf16[4,96,96]{2,1,0:T(8,128)(2,1)S(1)}, bf16[4,96,96]{2,1,0:T(8,128)(2,1)}, u32[]{:S(2)}) copy-start(bf16[4,96,96]{2,1,0:T(8,128)(2,1)} %param.10) | copy-start | bytes 221188
  6.5 50.0 %all-gather.3.cloned.1.call-start = ((), (), s32[]{:S(2)}) async-start(), calls=%async_computation.2 | async-start | bytes 1769472 | tf_op jit(solution)/shard_map/all_gather | solution.py:32
  7.3 83.4 %reduce-scatter.2.cloned.1.call-start = ((), (), s32[]{:S(2)}) async-start(), calls=%async_computation.1 | async-start | bytes 491520 | tf_op jit(solution)/shard_map/reduce_scatter | solution.py:39
  61.2 8.2 %copy-start.2 = (bf16[4,480,96]{1,2,0:T(8,128)(2,1)S(1)}, bf16[4,480,96]{1,2,0:T(8,128)(2,1)}, u32[]{:S(2)}) copy-start(bf16[4,480,96]{1,2,0:T(8,128)(2,1)} %param.11) | copy-start | bytes 1105924
  69.3 1.5 %copy-start.1 = (f32[3840]{0:T(1024)S(1)}, f32[3840]{0:T(1024)}, u32[]{:S(2)}) copy-start(f32[3840]{0:T(1024)} %param.13) | copy-start | bytes 46084
  69.4 1.5 %copy-start.4 = (s32[96]{0:T(128)S(1)}, s32[96]{0:T(128)}, u32[]{:S(2)}) copy-start(s32[96]{0:T(128)} %param.14) | copy-start | bytes 1156
  69.4 1.5 %copy-start.5 = (f32[96]{0:T(128)S(1)}, f32[96]{0:T(128)}, u32[]{:S(2)}) copy-start(f32[96]{0:T(128)} %param.12) | copy-start | bytes 1156
  69.4 1.9 %copy-start.3 = (s32[480]{0:T(512)S(1)}, s32[480]{0:T(512)}, u32[]{:S(2)}) copy-start(s32[480]{0:T(512)} %param.15) | copy-start | bytes 5764
Sparse Core Ops, SparseCore 0:
  9.5 46.9 all-gather.2
  70.9 19.6 reduce-scatter.1
where the time goes:
time: 99.3 us; the launch traced here: 99.1 us
  waiting for transfers between devices  40.8 us (41%)
  blocking collectives  23.2 us (23%)
  matrix products  14.3 us (14%)
  between operations  13.5 us (14%)
  local copies, waits for them, and re-layouts  5.52 us (6%)
  other arithmetic  1.63 us (2%)
    all_gather x1, waiting for transfers between devices, on_device(): lax.all_gather(trials, 'vrow', axis=1, tiled=True)  24.2 us
    psum x1, blocking collectives, on_device(): pair_sums = lax.psum(partial_pairs, 'vrow')  23.2 us
    reduce_scatter x1, waiting for transfers between devices, on_device(): lax.psum_scatter(combined, ('aux', 'grp'), scatter_dimension=0, tiled=True)  15.9 us
    dot_general x1, matrix products, on_device(): jnp.einsum('rb,qab->qra', lax.all_gather(trials, 'vrow', axis=1, tiled=Tr...  7.84 us
    dot_general x3, matrix products, table_lookup(): return jnp.dot(picker, table, precision=lax.Precision.HIGHEST)  3.86 us
    unnamed x14, local copies, waits for them, and re-layouts  2.42 us
    all_gather x1, local copies, waits for them, and re-layouts, on_device(): lax.all_gather(trials, 'vrow', axis=1, tiled=True)  2.27 us
  transfers between devices with their start and end apart: 2, of which 2 were waited for; matrix products, arithmetic and copies ran while one was open for 6% of the time, Pallas kernels for 0%

commit v1 on v0

--- a/solution.py
+++ b/solution.py
@@ -1,7 +1,17 @@
+import functools
+
 import jax
 import jax.numpy as jnp
 from jax import lax
+from jax.experimental import pallas as pl
+from jax.experimental.pallas import tpu as pltpu
 from jax.sharding import PartitionSpec as P
+
+MESH = pl.DeviceIdType.MESH
+F32 = jnp.float32
+BF16 = jnp.bfloat16
+LANES = 128
+PACK = 16
 
 
 def table_lookup(order, table):
@@ -10,7 +20,7 @@
     return jnp.dot(picker, table, precision=lax.Precision.HIGHEST)
 
 
-def on_device(
+def plain_on_device(
     trials, vv_factors, screened, ov_factors, occ_energy, virt_energy, occ_order, virt_order
 ):
     groups = lax.axis_size(("aux", "grp"))
@@ -45,6 +55,287 @@
     return summed + (virt_levels[None, :] - row_levels[:, None]) * own_trials
 
 
+def fused_kernel(
+    trials, vv_hbm, screened, ov_hbm, occ_energy, virt_energy, occ_order, virt_order,
+    out,
+    gathered, packed, vbuf, ovbuf, acc, screen_bd, combined, pair_buf, send_buf, recv_buf,
+    vv_sem, ov_sem, z_send, z_recv, x_send, x_recv, y_send, y_recv, c_send, c_recv,
+    p_send, p_recv, r_send, r_recv,
+):
+    rows, local = trials.shape
+    slabs = vv_hbm.shape[0]
+    occupied = occ_energy.shape[1]
+    count_trials = rows // occupied
+    half_cols = packed.shape[2]
+    quarter = rows // 4
+    half_rows = rows // 2
+    levels = gathered.shape[0] // 2
+
+    v = lax.axis_index("vrow")
+    y = lax.axis_index("aux")
+    c = lax.axis_index("grp")
+    z = v // 2
+    x = v % 2
+    half = z // 2
+    partner_z = {0: z, 1: z + 1 - 2 * (z % 2), 2: (z + 2) % 4, 3: 3 - z}
+
+    def row_id(zz, xx):
+        return zz * 2 + xx
+
+    mine = pl.ds(pl.multiple_of((2 * c + y) * quarter, PACK), quarter)
+    my_half = pl.ds(pl.multiple_of(c * half_rows, PACK), half_rows)
+
+    vv_copies = {}
+    for slot in range(2):
+        side = half if slot == 0 else 1 - half
+        cols = pl.ds(pl.multiple_of(side * half_cols, LANES), half_cols)
+        for q in range(slabs):
+            vv_copies[slot, q] = pltpu.make_async_copy(
+                vv_hbm.at[q, :, cols], vbuf.at[slot, q], vv_sem.at[slot, q]
+            )
+    ov_copy = pltpu.make_async_copy(ov_hbm, ovbuf, ov_sem)
+    ov_copy.start()
+    for q in range(slabs):
+        vv_copies[0, q].start()
+    for q in range(slabs):
+        vv_copies[1, q].start()
+
+    barrier = pltpu.get_barrier_semaphore()
+    peers = [(row_id(partner_z[d], xx), y, c) for d in range(4) for xx in (x, 1 - x)][1:]
+    group = [(v, 1 - y, c), (v, y, 1 - c), (v, 1 - y, 1 - c)]
+    for peer in peers + group:
+        pl.semaphore_signal(barrier, inc=1, device_id=peer, device_id_type=MESH)
+    pl.semaphore_wait(barrier, len(peers) + len(group))
+
+    def remote(src, dst, send, recv, peer):
+        return pltpu.make_async_remote_copy(
+            src_ref=src, dst_ref=dst, send_sem=send, recv_sem=recv,
+            device_id=peer, device_id_type=MESH,
+        )
+
+    z_copies, x_copies, y_copies, c_copies = {}, {}, {}, {}
+    to_x = (row_id(z, 1 - x), y, c)
+    to_y = (v, 1 - y, c)
+    to_c = (v, y, 1 - c)
+    for d in (1, 2, 3):
+        z_copies[d] = remote(
+            trials.at[mine], gathered.at[v, mine], z_send.at[d], z_recv.at[d],
+            (row_id(partner_z[d], x), y, c),
+        )
+    x_copies[0] = remote(
+        trials.at[my_half], gathered.at[v, my_half], x_send.at[0], x_recv.at[0], to_x
+    )
+    for d in (1, 2, 3):
+        same = gathered.at[row_id(partner_z[d], x)]
+        cross = gathered.at[row_id(partner_z[d], 1 - x)]
+        x_copies[d] = remote(same.at[mine], same.at[mine], x_send.at[d], x_recv.at[d], to_x)
+        for k, block in ((0, same), (1, cross)):
+            y_copies[d, k] = remote(
+                block.at[mine], block.at[mine], y_send.at[d, k], y_recv.at[d, k], to_y
+            )
+            c_copies[d, k] = remote(
+                block.at[my_half], block.at[my_half], c_send.at[d, k], c_recv.at[d, k], to_c
+            )
+    cross = gathered.at[row_id(z, 1 - x)]
+    c_copies[0, 1] = remote(
+        cross.at[my_half], cross.at[my_half], c_send.at[0, 1], c_recv.at[0, 1], to_c
+    )
+
+    for d in (3, 2, 1):
+        z_copies[d].start()
+    x_copies[0].start()
+
+    gathered[v] = trials[...]
+    ov_copy.wait()
+    split = [trials[t * occupied:(t + 1) * occupied, :].astype(F32) for t in range(count_trials)]
+    whole = (local // LANES) * LANES
+    pair_rows = []
+    for q in range(slabs):
+        factor = ovbuf[q].astype(F32)
+        for t in range(count_trials):
+            pair_rows.append(jnp.sum(factor * split[t], axis=0, keepdims=True))
+    pair_buf[0] = jnp.concatenate(pair_rows, axis=0)
+    p_copies = []
+    for k, peer in enumerate(peers):
+        p_copies.append(
+            remote(pair_buf.at[0], pair_buf.at[k + 1], p_send.at[k], p_recv.at[k], peer)
+        )
+        p_copies[-1].start()
+
+    for d in (1, 2, 3):
+        z_copies[d].wait_recv()
+        x_copies[d].start()
+        y_copies[d, 0].start()
+
+    screen_bd[...] = jnp.zeros(screen_bd.shape, screen_bd.dtype)
+    for q in range(slabs):
+        turned = screened[q].astype(F32).T.astype(BF16)
+        for t in range(count_trials):
+            span = slice(t * occupied, (t + 1) * occupied)
+            screen_bd[q, span, span] = turned
+
+    x_copies[0].wait_recv()
+    c_copies[0, 1].start()
+    for d in (1, 2, 3):
+        x_copies[d].wait_recv()
+        y_copies[d, 1].start()
+
+    blocks = virt_energy.shape[0]
+    order = virt_order[...]
+    picker = (order // LANES == lax.broadcasted_iota(jnp.int32, (blocks, local), 0)).astype(F32)
+    rows_of = lax.dot_general(
+        virt_energy[...].T, picker, (((1,), (0,)), ((), ())),
+        precision=lax.Precision.HIGHEST, preferred_element_type=F32,
+    )
+    lane_ids = lax.broadcasted_iota(jnp.int32, (LANES, local), 0)
+    virt_levels = jnp.sum(
+        jnp.where(order % LANES == lane_ids, rows_of, 0.0), axis=0, keepdims=True
+    )
+    share = out.shape[0]
+    owner = 2 * y + c
+    row_ids = owner * share + lax.broadcasted_iota(jnp.int32, (share, occupied), 0)
+    row_ids = row_ids % occupied
+    occ_ids = lax.broadcasted_iota(jnp.int32, (share, occupied), 1)
+    order_of = jnp.sum(
+        jnp.where(row_ids == occ_ids, occ_order[...].astype(F32), 0.0), axis=1, keepdims=True
+    ).astype(jnp.int32)
+    row_levels = jnp.sum(
+        jnp.where(order_of == occ_ids, occ_energy[...], 0.0), axis=1, keepdims=True
+    )
+    own_rows = pl.ds(pl.multiple_of(owner * share, PACK), share)
+    out[...] = (virt_levels - row_levels) * trials[own_rows, :].astype(F32)
+
+    y_copies[1, 0].wait_recv()
+    c_copies[1, 0].start()
+    y_copies[1, 1].wait_recv()
+    c_copies[1, 1].start()
+
+    for copy in p_copies:
+        copy.wait_recv()
+    pair_sums = 2.0 * jnp.sum(jnp.sum(pair_buf[...], axis=0), axis=1, keepdims=True)
+    for t in range(count_trials):
+        term = jnp.zeros((occupied, local), F32)
+        for q in range(slabs):
+            k = q * count_trials + t
+            term = term + ovbuf[q].astype(F32) * pair_sums[k:k + 1, :]
+        combined[t * occupied:(t + 1) * occupied, :] = term
+
+    def pack(slot):
+        side = half if slot == 0 else 1 - half
+        for s in range(half_cols // local):
+            packed[slot, :, s * local:(s + 1) * local] = gathered[side * (levels) + s]
+
+    def product(slot, q):
+        return lax.dot_general(
+            vbuf[slot, q], packed[slot], (((1,), (1,)), ((), ())), preferred_element_type=F32
+        )
+
+    for d in (2, 3):
+        for k in (0, 1):
+            y_copies[d, k].wait_recv()
+            c_copies[d, k].start()
+    c_copies[0, 1].wait_recv()
+    c_copies[1, 0].wait_recv()
+    c_copies[1, 1].wait_recv()
+    pack(0)
+    for q in range(slabs):
+        vv_copies[0, q].wait()
+        acc[q] = product(0, q)
+
+    for d in (2, 3):
+        for k in (0, 1):
+            c_copies[d, k].wait_recv()
+    pack(1)
+    total = combined[...]
+    for q in range(slabs):
+        vv_copies[1, q].wait()
+        image = (acc[q] + product(1, q)).astype(BF16)
+        total = total - lax.dot_general(
+            screen_bd[q], image, (((1,), (1,)), ((), ())), preferred_element_type=F32
+        )
+    combined[...] = total
+
+    r_copies = []
+    for k, (yy, cc) in enumerate(((1 - y, 1 - c), (1 - y, c), (y, 1 - c))):
+        theirs = pl.ds(pl.multiple_of((2 * yy + cc) * share, PACK), share)
+        send_buf[k] = combined[theirs, :].astype(BF16)
+        r_copies.append(
+            remote(send_buf.at[k], recv_buf.at[k], r_send.at[k], r_recv.at[k], (v, yy, cc))
+        )
+        r_copies[-1].start()
+    summed = out[...] + combined[own_rows, :]
+    for k in (2, 1, 0):
+        r_copies[k].wait_recv()
+        summed = summed + recv_buf[k].astype(F32)
+    out[...] = summed
+
+    everything = [*z_copies.values(), *x_copies.values(), *y_copies.values(), *c_copies.values()]
+    for copy in everything + p_copies + r_copies:
+        copy.wait_send()
+
+
+def fused_on_device(
+    trials, vv_factors, screened, ov_factors, occ_energy, virt_energy, occ_order, virt_order
+):
+    rows, local = trials.shape
+    slabs, _, virt = vv_factors.shape
+    occupied = occ_energy.shape[0]
+    count_trials = rows // occupied
+    parts = virt // local
+    share = rows // 4
+    vmem = pl.BlockSpec(memory_space=pltpu.VMEM)
+    anywhere = pl.BlockSpec(memory_space=pl.ANY)
+    dma = pltpu.SemaphoreType.DMA
+    return pl.pallas_call(
+        fused_kernel,
+        out_shape=jax.ShapeDtypeStruct((share, local), F32),
+        in_specs=[vmem, anywhere, vmem, anywhere, vmem, vmem, vmem, vmem],
+        out_specs=vmem,
+        scratch_shapes=[
+            pltpu.VMEM((parts, rows, local), BF16),
+            pltpu.VMEM((2, rows, virt // 2), BF16),
+            pltpu.VMEM((2, slabs, local, virt // 2), BF16),
+            pltpu.VMEM((slabs, occupied, local), BF16),
+            pltpu.VMEM((slabs, local, rows), F32),
+            pltpu.VMEM((slabs, rows, rows), BF16),
+            pltpu.VMEM((rows, local), F32),
+            pltpu.VMEM((parts, slabs * count_trials, local), F32),
+            pltpu.VMEM((3, share, local), BF16),
+            pltpu.VMEM((3, share, local), BF16),
+            dma((2, slabs)), dma,
+            dma((4,)), dma((4,)), dma((4,)), dma((4,)),
+            dma((4, 2)), dma((4, 2)), dma((4, 2)), dma((4, 2)),
+            dma((parts - 1,)), dma((parts - 1,)), dma((3,)), dma((3,)),
+        ],
+        compiler_params=pltpu.CompilerParams(
+            collective_id=0, has_side_effects=True, vmem_limit_bytes=56 * 1024 * 1024
+        ),
+    )(
+        trials,
+        vv_factors,
+        screened,
+        jnp.swapaxes(ov_factors, 1, 2),
+        occ_energy.reshape(1, occupied),
+        virt_energy.reshape(virt // LANES, LANES),
+        occ_order.reshape(1, occupied),
+        virt_order.reshape(1, local),
+    )
+
+
+def on_device(trials, vv_factors, *rest):
+    rows, local = trials.shape
+    virt = vv_factors.shape[2]
+    sizes = [lax.axis_size(name) for name in ("vrow", "aux", "grp")]
+    fits = (
+        sizes == [8, 2, 2]
+        and rows % (4 * PACK) == 0
+        and (virt // 2) % LANES == 0
+        and virt == sizes[0] * local
+    )
+    body = fused_on_device if fits else plain_on_device
+    return body(trials, vv_factors, *rest)
+
+
 def solution(mesh):
     placed = (
         P(None, "vrow"),

time: 99.3 us -> 38 us (0.38)
  waiting for transfers between devices: 40.8 us -> 0 us
  Pallas kernels: 0 us -> 36.3 us
  blocking collectives: 23.2 us -> 0 us
  matrix products: 14.3 us -> 0 us
  between operations: 13.5 us -> 0.01 us
  local copies, waits for them, and re-layouts: 5.52 us -> 1.54 us
  other arithmetic: 1.63 us -> 0 us
    pallas_call x0 -> x1, Pallas kernels: none -> 36.3 us  [fused_on_device(): pl.pallas_call(fused_kernel, out_shape=jax.ShapeDtypeStruct((share, local...]
    all_gather x1 -> x0, waiting for transfers between devices: 24.2 us -> none  [on_device(): lax.all_gather(trials, 'vrow', axis=1, tiled=True)]
    psum x1 -> x0, blocking collectives: 23.2 us -> none  [on_device(): pair_sums = lax.psum(partial_pairs, 'vrow')]
    reduce_scatter x1 -> x0, waiting for transfers between devices: 15.9 us -> none  [on_device(): lax.psum_scatter(combined, ('aux', 'grp'), scatter_dimension=0, tiled=True)]
    dot_general x7 -> x0, matrix products: 14.3 us -> none  [the longest x1 7.84 us: on_device(): jnp.einsum('rb,qab->qra', lax.all_gather(trials, 'vrow', axis=1, tiled=Tr...]
    all_gather x1 -> x0, local copies, waits for them, and re-layouts: 2.27 us -> none  [on_device(): lax.all_gather(trials, 'vrow', axis=1, tiled=True)]
    add x1 -> x0, other arithmetic: 1.62 us -> none  [on_device(): return summed + (virt_levels[None, :] - row_levels[:, None]) * own_trials]
    unnamed x14 -> x1, local copies, waits for them, and re-layouts: 2.42 us -> 1.54 us
  transfers between devices with their start and end apart: 2 -> 0, of which waited for: 2 -> 0; matrix products, arithmetic and copies ran while one was open for 6% -> 0% of each run, Pallas kernels for 0% -> 0%
where the time goes in v1:
time: 38 us; the launch traced here: 37.9 us
  Pallas kernels  36.3 us (96%)
  local copies, waits for them, and re-layouts  1.54 us (4%)
    pallas_call x1, Pallas kernels, fused_on_device(): pl.pallas_call(fused_kernel, out_shape=jax.ShapeDtypeStruct((share, local...  36.3 us
    unnamed x1, local copies, waits for them, and re-layouts  1.54 us

profile of v1, /device:TPU:0, one launch (start us, length us, event | category | flops | bytes accessed | tf_op | source)
XLA Modules:
  0.0 37.9 jit_solution(17596317139870243399)
XLA Ops:
  0.0 36.3 %shard_map.82 = f32[48,480]{1,0:T(8,128)} custom-call(bf16[192,480]{1,0:T(8,128)(2,1)} %trials.1, bf16[4,480,3840]{2,1,0:T(8,128)(2,1)} %vv_hbm.1, bf16[4,96,96]{2,1,0:T(8,128)(2,1)} %screened.1, bf16[4,96,480]{2,1,0:T(8,128)(2,1)} %bitcast.5, f32[1,96]{1,0:T(1,128)} %bitcast.8, f32[30,128]{1,0:T(8,128)} %bitcast.6, s32[1,96]{1,0:T(1,128)} %bitcast.9, ...), custom_call_target="tpu_custom_call" | custom-call | tf_op jit(solution)/shard_map/pallas_call | solution.py:289
  36.3 1.5 %copy.10 = f32[48,480]{1,0:T(8,128)} copy(f32[48,480]{1,0:T(8,128)} %shard_map.82) | data formatting | bytes 184320

commit v2 on v1

--- a/solution.py
+++ b/solution.py
@@ -56,13 +56,14 @@
 
 
 def fused_kernel(
-    trials, vv_hbm, screened, ov_hbm, occ_energy, virt_energy, occ_order, virt_order,
+    trials_hbm, vv_hbm, screened_hbm, ov_hbm, occ_e_hbm, virt_e_hbm, occ_o_hbm, virt_o_hbm,
     out,
+    screened, occ_energy, virt_energy, occ_order, virt_order,
     gathered, packed, vbuf, ovbuf, acc, screen_bd, combined, pair_buf, send_buf, recv_buf,
-    vv_sem, ov_sem, z_send, z_recv, x_send, x_recv, y_send, y_recv, c_send, c_recv,
+    vv_sem, in_sem, z_send, z_recv, x_send, x_recv, y_send, y_recv, c_send, c_recv,
     p_send, p_recv, r_send, r_recv,
 ):
-    rows, local = trials.shape
+    rows, local = trials_hbm.shape
     slabs = vv_hbm.shape[0]
     occupied = occ_energy.shape[1]
     count_trials = rows // occupied
@@ -84,6 +85,12 @@
 
     mine = pl.ds(pl.multiple_of((2 * c + y) * quarter, PACK), quarter)
     my_half = pl.ds(pl.multiple_of(c * half_rows, PACK), half_rows)
+
+    barrier = pltpu.get_barrier_semaphore()
+    peers = [(row_id(partner_z[d], xx), y, c) for d in range(4) for xx in (x, 1 - x)][1:]
+    group = [(v, 1 - y, c), (v, y, 1 - c), (v, 1 - y, 1 - c)]
+    for peer in peers + group:
+        pl.semaphore_signal(barrier, inc=1, device_id=peer, device_id_type=MESH)
 
     vv_copies = {}
     for slot in range(2):
@@ -93,18 +100,22 @@
             vv_copies[slot, q] = pltpu.make_async_copy(
                 vv_hbm.at[q, :, cols], vbuf.at[slot, q], vv_sem.at[slot, q]
             )
-    ov_copy = pltpu.make_async_copy(ov_hbm, ovbuf, ov_sem)
-    ov_copy.start()
+    trials = gathered.at[v]
+    in_copies = [
+        pltpu.make_async_copy(src, dst, in_sem.at[k])
+        for k, (src, dst) in enumerate((
+            (trials_hbm, trials), (ov_hbm, ovbuf), (screened_hbm, screened),
+            (occ_e_hbm, occ_energy), (virt_e_hbm, virt_energy),
+            (occ_o_hbm, occ_order), (virt_o_hbm, virt_order),
+        ))
+    ]
+    for copy in in_copies:
+        copy.start()
     for q in range(slabs):
         vv_copies[0, q].start()
     for q in range(slabs):
         vv_copies[1, q].start()
 
-    barrier = pltpu.get_barrier_semaphore()
-    peers = [(row_id(partner_z[d], xx), y, c) for d in range(4) for xx in (x, 1 - x)][1:]
-    group = [(v, 1 - y, c), (v, y, 1 - c), (v, 1 - y, 1 - c)]
-    for peer in peers + group:
-        pl.semaphore_signal(barrier, inc=1, device_id=peer, device_id_type=MESH)
     pl.semaphore_wait(barrier, len(peers) + len(group))
 
     def remote(src, dst, send, recv, peer):
@@ -119,11 +130,11 @@
     to_c = (v, y, 1 - c)
     for d in (1, 2, 3):
         z_copies[d] = remote(
-            trials.at[mine], gathered.at[v, mine], z_send.at[d], z_recv.at[d],
+            trials_hbm.at[mine], gathered.at[v, mine], z_send.at[d], z_recv.at[d],
             (row_id(partner_z[d], x), y, c),
         )
     x_copies[0] = remote(
-        trials.at[my_half], gathered.at[v, my_half], x_send.at[0], x_recv.at[0], to_x
+        trials_hbm.at[my_half], gathered.at[v, my_half], x_send.at[0], x_recv.at[0], to_x
     )
     for d in (1, 2, 3):
         same = gathered.at[row_id(partner_z[d], x)]
@@ -145,16 +156,16 @@
         z_copies[d].start()
     x_copies[0].start()
 
-    gathered[v] = trials[...]
-    ov_copy.wait()
+    for copy in in_copies:
+        copy.wait()
     split = [trials[t * occupied:(t + 1) * occupied, :].astype(F32) for t in range(count_trials)]
-    whole = (local // LANES) * LANES
     pair_rows = []
     for q in range(slabs):
         factor = ovbuf[q].astype(F32)
         for t in range(count_trials):
             pair_rows.append(jnp.sum(factor * split[t], axis=0, keepdims=True))
-    pair_buf[0] = jnp.concatenate(pair_rows, axis=0)
+    row_sums = jnp.sum(jnp.concatenate(pair_rows, axis=0), axis=1, keepdims=True)
+    pair_buf[0] = jnp.broadcast_to(row_sums, pair_buf.shape[1:])
     p_copies = []
     for k, peer in enumerate(peers):
         p_copies.append(
@@ -162,10 +173,18 @@
         )
         p_copies[-1].start()
 
-    for d in (1, 2, 3):
+    z_copies[1].wait_recv()
+    x_copies[1].start()
+    y_copies[1, 0].start()
+    x_copies[0].wait_recv()
+    c_copies[0, 1].start()
+    for d in (2, 3):
         z_copies[d].wait_recv()
         x_copies[d].start()
         y_copies[d, 0].start()
+    for d in (1, 2, 3):
+        x_copies[d].wait_recv()
+        y_copies[d, 1].start()
 
     screen_bd[...] = jnp.zeros(screen_bd.shape, screen_bd.dtype)
     for q in range(slabs):
@@ -174,11 +193,9 @@
             span = slice(t * occupied, (t + 1) * occupied)
             screen_bd[q, span, span] = turned
 
-    x_copies[0].wait_recv()
-    c_copies[0, 1].start()
-    for d in (1, 2, 3):
-        x_copies[d].wait_recv()
-        y_copies[d, 1].start()
+    for k in (0, 1):
+        y_copies[1, k].wait_recv()
+        c_copies[1, k].start()
 
     blocks = virt_energy.shape[0]
     order = virt_order[...]
@@ -205,14 +222,13 @@
     own_rows = pl.ds(pl.multiple_of(owner * share, PACK), share)
     out[...] = (virt_levels - row_levels) * trials[own_rows, :].astype(F32)
 
-    y_copies[1, 0].wait_recv()
-    c_copies[1, 0].start()
-    y_copies[1, 1].wait_recv()
-    c_copies[1, 1].start()
+    for d in (2, 3):
+        y_copies[d, 0].wait_recv()
+        c_copies[d, 0].start()
 
     for copy in p_copies:
         copy.wait_recv()
-    pair_sums = 2.0 * jnp.sum(jnp.sum(pair_buf[...], axis=0), axis=1, keepdims=True)
+    pair_sums = 2.0 * jnp.sum(pair_buf[...], axis=0)[:, :1]
     for t in range(count_trials):
         term = jnp.zeros((occupied, local), F32)
         for q in range(slabs):
@@ -227,13 +243,9 @@
 
     def product(slot, q):
         return lax.dot_general(
-            vbuf[slot, q], packed[slot], (((1,), (1,)), ((), ())), preferred_element_type=F32
-        )
-
-    for d in (2, 3):
-        for k in (0, 1):
-            y_copies[d, k].wait_recv()
-            c_copies[d, k].start()
+            packed[slot], vbuf[slot, q], (((1,), (1,)), ((), ())), preferred_element_type=F32
+        )
+
     c_copies[0, 1].wait_recv()
     c_copies[1, 0].wait_recv()
     c_copies[1, 1].wait_recv()
@@ -241,6 +253,9 @@
     for q in range(slabs):
         vv_copies[0, q].wait()
         acc[q] = product(0, q)
+        if q < 2:
+            y_copies[q + 2, 1].wait_recv()
+            c_copies[q + 2, 1].start()
 
     for d in (2, 3):
         for k in (0, 1):
@@ -251,7 +266,7 @@
         vv_copies[1, q].wait()
         image = (acc[q] + product(1, q)).astype(BF16)
         total = total - lax.dot_general(
-            screen_bd[q], image, (((1,), (1,)), ((), ())), preferred_element_type=F32
+            screen_bd[q], image, (((1,), (0,)), ((), ())), preferred_element_type=F32
         )
     combined[...] = total
 
@@ -289,20 +304,25 @@
     return pl.pallas_call(
         fused_kernel,
         out_shape=jax.ShapeDtypeStruct((share, local), F32),
-        in_specs=[vmem, anywhere, vmem, anywhere, vmem, vmem, vmem, vmem],
+        in_specs=[anywhere] * 8,
         out_specs=vmem,
         scratch_shapes=[
+            pltpu.VMEM((slabs, occupied, occupied), BF16),
+            pltpu.VMEM((1, occupied), F32),
+            pltpu.VMEM((virt // LANES, LANES), F32),
+            pltpu.VMEM((1, occupied), jnp.int32),
+            pltpu.VMEM((1, local), jnp.int32),
             pltpu.VMEM((parts, rows, local), BF16),
             pltpu.VMEM((2, rows, virt // 2), BF16),
             pltpu.VMEM((2, slabs, local, virt // 2), BF16),
             pltpu.VMEM((slabs, occupied, local), BF16),
-            pltpu.VMEM((slabs, local, rows), F32),
+            pltpu.VMEM((slabs, rows, local), F32),
             pltpu.VMEM((slabs, rows, rows), BF16),
             pltpu.VMEM((rows, local), F32),
-            pltpu.VMEM((parts, slabs * count_trials, local), F32),
+            pltpu.VMEM((parts, slabs * count_trials, LANES), F32),
             pltpu.VMEM((3, share, local), BF16),
             pltpu.VMEM((3, share, local), BF16),
-            dma((2, slabs)), dma,
+            dma((2, slabs)), dma((7,)),
             dma((4,)), dma((4,)), dma((4,)), dma((4,)),
             dma((4, 2)), dma((4, 2)), dma((4, 2)), dma((4, 2)),
             dma((parts - 1,)), dma((parts - 1,)), dma((3,)), dma((3,)),
@@ -328,6 +348,7 @@
     sizes = [lax.axis_size(name) for name in ("vrow", "aux", "grp")]
     fits = (
         sizes == [8, 2, 2]
+        and vv_factors.shape[0] >= 2
         and rows % (4 * PACK) == 0
         and (virt // 2) % LANES == 0
         and virt == sizes[0] * local

time: 38 us -> 32 us (0.84)
  Pallas kernels: 36.3 us -> 30.3 us
    pallas_call x1, Pallas kernels: 36.3 us -> 30.3 us  [fused_on_device(): pl.pallas_call(fused_kernel, out_shape=jax.ShapeDtypeStruct((share, local...]
where the time goes in v2:
time: 32 us; the launch traced here: 31.8 us
  Pallas kernels  30.3 us (95%)
  local copies, waits for them, and re-layouts  1.54 us (5%)
    pallas_call x1, Pallas kernels, fused_on_device(): pl.pallas_call(fused_kernel, out_shape=jax.ShapeDtypeStruct((share, local...  30.3 us
    unnamed x1, local copies, waits for them, and re-layouts  1.54 us

profile of v2, /device:TPU:0, one launch (start us, length us, event | category | flops | bytes accessed | tf_op | source)
XLA Modules:
  0.0 31.8 jit_solution(3797118960017171708)
XLA Ops:
  0.0 30.3 %shard_map.82 = f32[48,480]{1,0:T(8,128)} custom-call(bf16[192,480]{1,0:T(8,128)(2,1)} %trials_hbm.1, bf16[4,480,3840]{2,1,0:T(8,128)(2,1)} %vv_hbm.1, bf16[4,96,96]{2,1,0:T(8,128)(2,1)} %screened_hbm.1, bf16[4,96,480]{2,1,0:T(8,128)(2,1)} %bitcast.5, f32[1,96]{1,0:T(1,128)} %bitcast.8, f32[30,128]{1,0:T(8,128)} %bitcast.6, s32[1,96]{1,0:T(1,128)} %bitcast.9, ...), custom_call_target="tpu_custom_call" | custom-call | tf_op jit(solution)/shard_map/pallas_call | solution.py:304
  30.3 1.5 %copy.10 = f32[48,480]{1,0:T(8,128)} copy(f32[48,480]{1,0:T(8,128)} %shard_map.82) | data formatting | bytes 184320
